TPU v7x, 256 devices: a whole 4x4x8 slice. The times are simulated.
256 devices in a mesh: rep: 64 (over y, z_lo, x, core), fsdp: 4 (over z_hi).
Axes of the slice: x: 4, y: 4, z: 8 (z_hi: 4, z_lo: 2; z = z_hi * 2 + z_lo), core: 2. Of those that a mesh axis runs over, the one named last changes fastest.
Arguments:
- tokens: bfloat16 [64, 960, 8192], P('rep', 'fsdp'), may hold values from -6 to 6
- key_proj: bfloat16 [64, 8192, 512], P('rep', 'fsdp'), may hold values from -0.0625 to 0.0625
- cotangent: bfloat16 [64, 960, 512], P('rep', 'fsdp'), may hold values from -0.59765625 to 0.59765625
- codes: int32 [64, 131072], P('rep', 'fsdp'), may hold values from -127 to 127
- block_scales: float32 [64, 1024], P('rep', 'fsdp'), may hold values from 0.002 to 0.02
- outer_params: float32 [131072], P('fsdp'), may hold values from -6 to 6
- outer_moment: float32 [131072], P('fsdp'), may hold values from -3 to 3
Outputs:
- grad_proj: bfloat16 [64, 8192, 512], P('rep', 'fsdp')
- input_grad: bfloat16 [64, 960, 8192], P('rep', 'fsdp')
- new_params: float32 [131072], P('fsdp')
- new_moment: float32 [131072], P('fsdp')
All inputs are finite; a program needn't handle non-finite values.
Results may differ from a plain program's by a relative error of at most 0.013.
Values may be sent and summed in bfloat16 or wider, within the bound.
A program may use at most 128 MiB of HBM per device.

v0:
```python
import jax
import jax.numpy as jnp
from jax import lax
from jax.sharding import PartitionSpec as P

BLOCK = 128


outer_rate = 0.7
outer_momentum = 0.9


def contract_rows(first_part, second_part):
    return lax.dot_general(
        first_part, second_part, (((0,), (0,)), ((), ())), preferred_element_type=jnp.float32
    )


def contract_cols(first_part, second_part):
    return lax.dot_general(
        first_part, second_part, (((1,), (1,)), ((), ())), preferred_element_type=jnp.float32
    )


def outer_step(outer_delta, params_part, moment_part):
    moment_next = outer_momentum * moment_part + outer_delta
    params_next = params_part - outer_rate * (outer_delta + outer_momentum * moment_next)
    return (params_next, moment_next)


def local(tokens, key_proj, cotangent, codes, block_scales, outer_params, outer_moment):
    inputs = tokens[0]
    weights = key_proj[0]
    upstream = cotangent[0]
    input_grads = contract_cols(
        upstream, lax.all_gather(weights, "fsdp", axis=0, tiled=True)
    ).astype(jnp.bfloat16)
    summed = lax.psum_scatter(
        contract_rows(inputs, upstream).astype(jnp.bfloat16),
        "fsdp",
        scatter_dimension=0,
        tiled=True,
    )
    grad_weights = summed[None]
    input_out = input_grads[None]
    dequant = (codes[0].reshape(-1, BLOCK).astype(jnp.float32) * block_scales[0][:, None]).reshape(
        -1
    )
    replicas = lax.axis_size("rep")
    total_sum = lax.psum(dequant, "rep")
    new_params, new_moment = outer_step(total_sum / replicas, outer_params, outer_moment)
    return (grad_weights, input_out, new_params, new_moment)


def solution(mesh):
    return jax.shard_map(
        local,
        mesh=mesh,
        in_specs=(
            P("rep", "fsdp", None),
            P("rep", "fsdp", None),
            P("rep", "fsdp", None),
            P("rep", "fsdp"),
            P("rep", "fsdp"),
            P("fsdp"),
            P("fsdp"),
        ),
        out_specs=(P("rep", "fsdp", None), P("rep", "fsdp", None), P("fsdp"), P("fsdp")),
        check_vma=False,
    )
```

profile of v0, /device:TPU:1, one launch (start us, length us, event | category | flops | bytes accessed | tf_op | source)
XLA Modules:
  0.0 742.1 jit_solution(12357456048344218921)
XLA Ops:
  8.0 0.0 copy-start
  8.0 0.0 all-reduce.2.cloned.1.call-start
  8.1 1.1 convert_element_type.15
  9.1 1.4 bitcast_multiply_fusion
  10.6 0.0 all-reduce.2.cloned.1.call-update
  10.6 0.0 all-gather.3.cloned.1.call-start
  10.6 0.5 all-gather.3.cloned.1.call-update
  11.2 0.0 reduce-scatter.2.cloned.1.call-start
  11.2 0.0 copy-done
  11.2 7.8 %convolution_convert_fusion = bf16[8192,512]{1,0:T(8,128)(2,1)} fusion(bf16[1,240,8192]{2,1,0:T(8,128)(2,1)} %param.7, bf16[1,240,512]{2,1,0:T(8,128)(2,1)S(1)} %copy-done), kind=kOutput, calls=%fused_computation | convolution fusion | flops 2017460224 | bytes 12566528 | tf_op jit(solution)/shard_map/dot_general | solution.py:14
  19.0 0.0 copy-start.1
  19.0 0.0 copy-start.2
  19.0 0.0 reduce-scatter.2.cloned.1.call-update
  19.0 706.3 %all-reduce.2.cloned.1.call-done = f32[32768]{0:T(1024)} async-done(((f32[32768]{0:T(1024)}), f32[32768]{0:T(1024)}) %all-reduce.2.cloned.1.call-update) | async-done | bytes 131088 | tf_op jit(solution)/shard_map/psum | solution.py:50
  725.3 0.0 copy-done.1
  725.3 0.0 copy-done.2
  725.3 1.6 multiply_subtract_fusion
  727.0 0.0 all-gather.3.cloned.1.call-done
  727.0 7.7 %fusion = bf16[1,240,8192]{2,1,0:T(8,128)(2,1)} fusion(bf16[1,8192,512]{2,1,0:T(8,128)(2,1)} %all-gather.3.cloned.1.call-done, bf16[1,240,512]{2,1,0:T(8,128)(2,1)S(1)} %copy-done), kind=kOutput, calls=%fused_computation.2 | convolution fusion | flops 2015232000 | bytes 12566528 | tf_op jit(solution)/shard_map/dot_general | solution.py:20
  734.7 0.0 reduce-scatter.2.cloned.1.call-done
Async XLA Ops:
  8.0 3.2 copy-start
  8.0 717.3 %all-reduce.2.cloned.1.call-start = ((), (), s32[]{:S(2)}) async-start(), calls=%async_computation.2 | async-start | bytes 262144 | tf_op jit(solution)/shard_map/psum | solution.py:50
  10.6 716.4 %all-gather.3.cloned.1.call-start = ((), (), s32[]{:S(2)}) async-start(), calls=%async_computation.3 | async-start | bytes 10485760 | tf_op jit(solution)/shard_map/all_gather | solution.py:36
  11.2 723.5 %reduce-scatter.2.cloned.1.call-start = ((), (), s32[]{:S(2)}) async-start(), calls=%async_computation.1 | async-start | bytes 10485760 | tf_op jit(solution)/shard_map/reduce_scatter | solution.py:38
  19.0 706.3 %copy-start.1 = (f32[32768]{0:T(1024)S(1)}, f32[32768]{0:T(1024)}, u32[]{:S(2)}) copy-start(f32[32768]{0:T(1024)} %param.12) | copy-start | bytes 393220
  19.0 706.3 %copy-start.2 = (f32[32768]{0:T(1024)S(1)}, f32[32768]{0:T(1024)}, u32[]{:S(2)}) copy-start(f32[32768]{0:T(1024)} %param.13) | copy-start | bytes 393220
Sparse Core Ops, SparseCore 0:
  12.0 713.2 all-reduce.1
Sparse Core Ops, SparseCore 1:
  12.9 159.2 all-gather.2
  175.2 151.1 reduce-scatter.1
where the time goes:
time: 742 us
  waiting for transfers between devices  707 us (95%)
  matrix products  15.5 us (2%)
  between operations  15.5 us (2%)
    psum x1, waiting for transfers between devices, local(): total_sum = lax.psum(dequant, 'rep')  706 us
  transfers between devices with their start and end apart: 3, of which 1 were waited for; matrix products, arithmetic and copies ran while one was open for 2% of the time, Pallas kernels for 0%

commit v1 on v0

v1 whole, which is shorter than its diff:
```python
import functools

import jax
import jax.numpy as jnp
from jax import lax
from jax.experimental import pallas as pl
from jax.experimental.pallas import tpu as pltpu
from jax.sharding import PartitionSpec as P

BLOCK = 128
TOK = 240
KV = 512
COLS = 2048
NF = 4
OUTER_RATE = 0.7
OUTER_MOMENTUM = 0.9

WIDTH = 512
CHUNKS = COLS // WIDTH
UPPER = 128
ROWS = 256
GA = 8
GB = 8
RA = ROWS // GA
RB = RA // GB

MESH = pl.DeviceIdType.MESH


def kernel(
    tok_hbm, kp_hbm, cot_hbm, codes_hbm, scales_hbm, params_hbm, moment_hbm,
    gp_out, ig_out, np_out, nm_out,
    tok, kp, cot, ig, gp, codes, scales, params, moment,
    deq, part_a, mine_b, part_b, sum_b, full_b, sum_a, full_a,
    load_sem, store_sem,
    c_send, c_recv, f_send, f_recv,
    t_send, t_recv, i_send, i_recv,
    a_send, a_recv, b_send, b_recv, gb_send, gb_recv, ga_send, ga_recv,
):
    rep = lax.axis_index("rep")
    me = lax.axis_index("fsdp")
    a_id = lax.rem(rep, GA)
    b_id = lax.div(rep, GA)

    def peer(d):
        return lax.rem(me + d, NF)

    def fs_dev(d):
        return (rep, peer(d))

    def a_peer(k):
        return lax.rem(a_id + k, GA)

    def b_peer(k):
        return lax.rem(b_id + k, GB)

    def a_dev(k):
        return (b_id * GA + a_peer(k), me)

    def b_dev(k):
        return (b_peer(k) * GA + a_id, me)

    def remote(src, dst, send, recv, dev):
        return pltpu.make_async_remote_copy(
            src_ref=src, dst_ref=dst, send_sem=send, recv_sem=recv,
            device_id=dev, device_id_type=MESH,
        )

    barrier = pltpu.get_barrier_semaphore()
    devs = [fs_dev(d) for d in (2, 1, 3)]
    devs += [b_dev(k) for k in range(1, GB)] + [a_dev(k) for k in range(1, GA)]
    for dev in devs:
        pl.semaphore_signal(barrier, inc=1, device_id=dev, device_id_type=MESH)

    loads = [
        pltpu.make_async_copy(cot_hbm, cot.at[me], load_sem.at[0]),
        pltpu.make_async_copy(kp_hbm, kp, load_sem.at[1]),
        pltpu.make_async_copy(codes_hbm, codes, load_sem.at[2]),
        pltpu.make_async_copy(scales_hbm, scales, load_sem.at[3]),
        pltpu.make_async_copy(params_hbm, params, load_sem.at[4]),
        pltpu.make_async_copy(moment_hbm, moment, load_sem.at[5]),
        pltpu.make_async_copy(
            tok_hbm.at[:, pl.ds(pl.multiple_of(me * COLS, COLS), COLS)], tok.at[me], load_sem.at[6]
        ),
    ]
    for load in loads:
        load.start()

    pl.semaphore_wait(barrier, len(devs))

    c_copies = [
        remote(cot_hbm, cot.at[me], c_send.at[k], c_recv.at[k], fs_dev(d))
        for k, d in enumerate((1, 3))
    ]
    for copy in c_copies:
        copy.start()

    def token_copy(k, d, c):
        start = pl.multiple_of(peer(d) * COLS + c * WIDTH, WIDTH)
        return remote(
            tok_hbm.at[:, pl.ds(start, WIDTH)],
            tok.at[me, :, pl.ds(c * WIDTH, WIDTH)],
            t_send.at[k, c], t_recv.at[k, c], fs_dev(d),
        )

    t_copies = [[token_copy(k, d, c) for k, d in enumerate((2, 1, 3))] for c in range(CHUNKS)]
    for copy in t_copies[0]:
        copy.start()

    loads[2].wait()
    loads[3].wait()
    spread = jnp.transpose(jnp.broadcast_to(scales[...], (BLOCK, ROWS)))
    deq[...] = codes[...].astype(jnp.float32) * spread
    a_copies = []
    for k in range(1, GA):
        rows = pl.ds(pl.multiple_of(a_peer(k) * RA, RA), RA)
        copy = remote(deq.at[rows], part_a.at[k - 1], a_send.at[k - 1], a_recv.at[k - 1], a_dev(k))
        copy.start()
        a_copies.append(copy)

    f_copies = []
    for k, (origin, target, lo, n) in enumerate(((3, 1, 0, UPPER), (1, 3, UPPER, TOK - UPPER))):
        c_copies[k].wait_recv()
        part = cot.at[peer(origin), pl.ds(lo, n)]
        copy = remote(part, part, f_send.at[k], f_recv.at[k], fs_dev(target))
        copy.start()
        f_copies.append(copy)

    for c in range(1, CHUNKS):
        for copy in t_copies[c]:
            copy.start()

    loads[0].wait()
    loads[1].wait()

    def product(d, slot, c):
        cols = pl.ds(c * WIDTH, WIDTH)
        ig[slot, :, cols] = lax.dot_general(
            cot[peer(d)], kp[cols, :], (((1,), (1,)), ((), ())),
            preferred_element_type=jnp.float32,
        ).astype(jnp.bfloat16)

    i_copies = []

    def send_products(d, slot):
        for c in range(CHUNKS):
            product(d, slot, c)
            start = pl.multiple_of(me * COLS + c * WIDTH, WIDTH)
            copy = remote(
                ig.at[slot, :, pl.ds(c * WIDTH, WIDTH)],
                ig_out.at[:, pl.ds(start, WIDTH)],
                i_send.at[slot, c], i_recv.at[slot, c], fs_dev(d),
            )
            copy.start()
            i_copies.append(copy)

    send_products(1, 1)
    send_products(3, 2)

    for copy in a_copies:
        copy.wait_recv()
    total = deq[pl.ds(pl.multiple_of(a_id * RA, RA), RA)]
    for k in range(GA - 1):
        total = total + part_a[k]
    for b in range(GB):
        mine_b[b] = total[b * RB:(b + 1) * RB]
    b_copies = []
    for k in range(1, GB):
        copy = remote(mine_b.at[b_peer(k)], part_b.at[k - 1], b_send.at[k - 1], b_recv.at[k - 1], b_dev(k))
        copy.start()
        b_copies.append(copy)

    for copy in f_copies:
        copy.wait_recv()
    send_products(2, 0)

    for copy in b_copies:
        copy.wait_recv()
    total = mine_b[b_id]
    for k in range(GB - 1):
        total = total + part_b[k]
    sum_b[...] = total
    full_b[b_id] = total
    gb_copies = []
    for k in range(1, GB):
        copy = remote(sum_b, full_b.at[b_id], gb_send.at[k - 1], gb_recv.at[k - 1], b_dev(k))
        copy.start()
        gb_copies.append(copy)

    stores = []
    for c in range(CHUNKS):
        product(0, 3, c)
    start = pl.multiple_of(me * COLS, COLS)
    store = pltpu.make_async_copy(ig.at[3], ig_out.at[:, pl.ds(start, COLS)], store_sem.at[0])
    store.start()
    stores.append(store)

    for copy in gb_copies:
        copy.wait_recv()
    for b in range(GB):
        sum_a[b * RB:(b + 1) * RB] = full_b[b]
    full_a[a_id] = sum_a[...]
    ga_copies = []
    for k in range(1, GA):
        copy = remote(sum_a, full_a.at[a_id], ga_send.at[k - 1], ga_recv.at[k - 1], a_dev(k))
        copy.start()
        ga_copies.append(copy)

    loads[4].wait()
    loads[5].wait()
    loads[6].wait()
    for copy in ga_copies:
        copy.wait_recv()
    delta = full_a[...].reshape(ROWS, BLOCK) / (GA * GB)
    moment_next = OUTER_MOMENTUM * moment[...] + delta
    params[...] = params[...] - OUTER_RATE * (delta + OUTER_MOMENTUM * moment_next)
    moment[...] = moment_next
    for k, (src, dst) in enumerate(((params, np_out), (moment, nm_out))):
        store = pltpu.make_async_copy(src, dst, store_sem.at[1 + k])
        store.start()
        stores.append(store)

    for c in range(CHUNKS):
        for copy in t_copies[c]:
            copy.wait_recv()
        cols = pl.ds(c * WIDTH, WIDTH)
        gp[cols, :] = lax.dot_general(
            tok[:, :, cols].reshape(NF * TOK, WIDTH), cot[...].reshape(NF * TOK, KV),
            (((0,), (0,)), ((), ())), preferred_element_type=jnp.float32,
        ).astype(jnp.bfloat16)
        store = pltpu.make_async_copy(gp.at[cols], gp_out.at[cols], store_sem.at[3 + c])
        store.start()
        stores.append(store)

    for copy in i_copies:
        copy.wait_recv()
    for store in stores:
        store.wait()
    sends = c_copies + f_copies + i_copies + a_copies + b_copies + gb_copies + ga_copies
    for row in t_copies:
        sends += row
    for copy in sends:
        copy.wait_send()


def local(tokens, key_proj, cotangent, codes, block_scales, outer_params, outer_moment):
    f32, bf16 = jnp.float32, jnp.bfloat16
    any_spec = pl.BlockSpec(memory_space=pl.ANY)
    dma = pltpu.SemaphoreType.DMA
    vmem = pltpu.VMEM
    grad_proj, input_grad, new_params, new_moment = pl.pallas_call(
        kernel,
        out_shape=(
            jax.ShapeDtypeStruct((COLS, KV), bf16),
            jax.ShapeDtypeStruct((TOK, NF * COLS), bf16),
            jax.ShapeDtypeStruct((ROWS, BLOCK), f32),
            jax.ShapeDtypeStruct((ROWS, BLOCK), f32),
        ),
        in_specs=[any_spec] * 7,
        out_specs=(any_spec,) * 4,
        scratch_shapes=[
            vmem((NF, TOK, COLS), bf16),
            vmem((COLS, KV), bf16),
            vmem((NF, TOK, KV), bf16),
            vmem((NF, TOK, COLS), bf16),
            vmem((COLS, KV), bf16),
            vmem((ROWS, BLOCK), jnp.int32),
            vmem((1, ROWS), f32),
            vmem((ROWS, BLOCK), f32),
            vmem((ROWS, BLOCK), f32),
            vmem((ROWS, BLOCK), f32),
            vmem((GA - 1, RA, BLOCK), f32),
            vmem((GB, RB, BLOCK), f32),
            vmem((GB - 1, RB, BLOCK), f32),
            vmem((RB, BLOCK), f32),
            vmem((GB, RB, BLOCK), f32),
            vmem((RA, BLOCK), f32),
            vmem((GA, RA, BLOCK), f32),
            dma((7,)),
            dma((3 + CHUNKS,)),
            dma((2,)), dma((2,)), dma((2,)), dma((2,)),
            dma((3, CHUNKS)), dma((3, CHUNKS)), dma((3, CHUNKS)), dma((3, CHUNKS)),
            dma((GA - 1,)), dma((GA - 1,)), dma((GB - 1,)), dma((GB - 1,)),
            dma((GB - 1,)), dma((GB - 1,)), dma((GA - 1,)), dma((GA - 1,)),
        ],
        compiler_params=pltpu.CompilerParams(
            collective_id=0, has_side_effects=True, vmem_limit_bytes=56 * 1024 * 1024
        ),
        name="step",
    )(
        tokens[0], key_proj[0], cotangent[0], codes.reshape(ROWS, BLOCK), block_scales,
        outer_params.reshape(ROWS, BLOCK), outer_moment.reshape(ROWS, BLOCK),
    )
    return grad_proj[None], input_grad[None], new_params.reshape(-1), new_moment.reshape(-1)


def solution(mesh):
    return jax.shard_map(
        local,
        mesh=mesh,
        in_specs=(
            P("rep", "fsdp", None),
            P("rep", "fsdp", None),
            P("rep", "fsdp", None),
            P("rep", "fsdp"),
            P("rep", "fsdp"),
            P("fsdp"),
            P("fsdp"),
        ),
        out_specs=(P("rep", "fsdp", None), P("rep", "fsdp", None), P("fsdp"), P("fsdp")),
        check_vma=False,
    )
```

time: 742 us -> 214 us (0.29)
  waiting for transfers between devices: 707 us -> 0 us
  Pallas kernels: 0 us -> 207 us
  matrix products: 15.5 us -> 0 us
  between operations: 15.5 us -> 0.65 us
    psum x1 -> x0, waiting for transfers between devices: 706 us -> none  [local(): total_sum = lax.psum(dequant, 'rep')]
    pallas_call x0 -> x1, Pallas kernels: none -> 207 us  [local(): pl.pallas_call(kernel, out_shape=(jax.ShapeDtypeStruct((COLS, KV), bf16),...]
    dot_general x2 -> x0, matrix products: 15.5 us -> none  [the longest x1 7.79 us: contract_rows(): lax.dot_general(first_part, second_part, (((0,), (0,)), ((), ())), prefer...]
  transfers between devices with their start and end apart: 3 -> 0, of which waited for: 1 -> 0; matrix products, arithmetic and copies ran while one was open for 2% -> 0% of each run, Pallas kernels for 0% -> 0%
where the time goes in v1:
time: 214 us
  Pallas kernels  207 us (97%)
  local copies, waits for them, and re-layouts  6.46 us (3%)
    pallas_call x1, Pallas kernels, local(): pl.pallas_call(kernel, out_shape=(jax.ShapeDtypeStruct((COLS, KV), bf16),...  207 us
    unnamed x10, local copies, waits for them, and re-layouts  6.46 us

profile of v1, /device:TPU:1, one launch (start us, length us, event | category | flops | bytes accessed | tf_op | source)
XLA Modules:
  0.0 214.4 jit_solution(17704848289390656468)
XLA Ops:
  0.6 207.3 %step.1 = (bf16[2048,512]{1,0:T(8,128)(2,1)}, bf16[240,8192]{1,0:T(8,128)(2,1)}, f32[256,128]{1,0:T(8,128)}, f32[256,128]{1,0:T(8,128)}) custom-call(bf16[240,8192]{1,0:T(8,128)(2,1)} %bitcast.10, bf16[2048,512]{1,0:T(8,128)(2,1)} %bitcast.12, bf16[240,512]{1,0:T(8,128)(2,1)} %bitcast.14, s32[256,128]{1,0:T(8,128)} %bitcast.15, f32[1,256]{1,0:T(1,128)} %scales_hbm.1, ...), custom_call_target="tpu_custom_call" | custom-call | tf_op jit(solution)/shard_map/step/pallas_call | solution.py:251
  207.9 0.0 copy-start
  207.9 3.2 %copy.15 = bf16[1,2048,512]{2,1,0:T(8,128)(2,1)} copy(bf16[1,2048,512]{2,1,0:T(8,128)(2,1)} %bitcast.13) | data formatting | bytes 4194304
  211.1 0.0 copy-done
  211.1 0.0 copy-start.2
  211.1 0.0 copy-start.1
  211.1 1.9 copy.16
  213.1 0.0 copy-done.2
  213.1 0.7 copy.17
  213.7 0.0 copy-done.1
  213.7 0.7 copy.18
Async XLA Ops:
  207.9 3.2 %copy-start = (bf16[240,8192]{1,0:T(8,128)(2,1)S(1)}, bf16[240,8192]{1,0:T(8,128)(2,1)}, u32[]{:S(2)}) copy-start(bf16[240,8192]{1,0:T(8,128)(2,1)} %get-tuple-element.9) | copy-start | bytes 11796484
  211.1 1.9 copy-start.2
  211.1 2.6 %copy-start.1 = (f32[256,128]{1,0:T(8,128)S(1)}, f32[256,128]{1,0:T(8,128)}, u32[]{:S(2)}) copy-start(f32[256,128]{1,0:T(8,128)} %get-tuple-element.11) | copy-start | bytes 393220

commit v2 on v1

v2 whole, which is shorter than its diff:
```python
import functools

import jax
import jax.numpy as jnp
from jax import lax
from jax.experimental import pallas as pl
from jax.experimental.pallas import tpu as pltpu
from jax.sharding import PartitionSpec as P

BLOCK = 128
TOK = 240
KV = 512
COLS = 2048
NF = 4
OUTER_RATE = 0.7
OUTER_MOMENTUM = 0.9

WIDTH = 256
CHUNKS = COLS // WIDTH
T_CUTS = ((0, 256), (256, 256), (512, 256), (768, 1280))
I_CUTS = ((0, 2048),)
UPPER = 128
ROWS = 256
GA = 8
GB = 8
RA = ROWS // GA
RB = RA // GB

ORDER = (2, 1, 3)

MESH = pl.DeviceIdType.MESH


def kernel(
    tok_hbm, kp_hbm, cot_hbm, codes_hbm, scales_hbm, params_hbm, moment_hbm,
    gp_out, ig_out, np_out, nm_out,
    tok, kp, cot, ig, codes, scales, params, moment,
    deq, part_a, mine_b, part_b, sum_b, full_b, sum_a, full_a,
    load_sem,
    c_send, c_recv, f_send, f_recv,
    t_send, t_recv, i_send, i_recv,
    a_send, a_recv, b_send, b_recv, gb_send, gb_recv, ga_send, ga_recv,
):
    rep = lax.axis_index("rep")
    me = lax.axis_index("fsdp")
    a_id = lax.rem(rep, GA)
    b_id = lax.div(rep, GA)

    def peer(d):
        return lax.rem(me + d, NF)

    def fs_dev(d):
        return (rep, peer(d))

    def a_peer(k):
        return lax.rem(a_id + k, GA)

    def b_peer(k):
        return lax.rem(b_id + k, GB)

    def a_dev(k):
        return (b_id * GA + a_peer(k), me)

    def b_dev(k):
        return (b_peer(k) * GA + a_id, me)

    def remote(src, dst, send, recv, dev):
        return pltpu.make_async_remote_copy(
            src_ref=src, dst_ref=dst, send_sem=send, recv_sem=recv,
            device_id=dev, device_id_type=MESH,
        )

    barrier = pltpu.get_barrier_semaphore()
    devs = [fs_dev(d) for d in ORDER]
    devs += [b_dev(k) for k in range(1, GB)] + [a_dev(k) for k in range(1, GA)]
    for dev in devs:
        pl.semaphore_signal(barrier, inc=1, device_id=dev, device_id_type=MESH)

    loads = [
        pltpu.make_async_copy(cot_hbm, cot.at[me], load_sem.at[0]),
        pltpu.make_async_copy(kp_hbm, kp, load_sem.at[1]),
        pltpu.make_async_copy(codes_hbm, codes, load_sem.at[2]),
        pltpu.make_async_copy(scales_hbm, scales, load_sem.at[3]),
        pltpu.make_async_copy(params_hbm, params, load_sem.at[4]),
        pltpu.make_async_copy(moment_hbm, moment, load_sem.at[5]),
        pltpu.make_async_copy(
            tok_hbm.at[:, pl.ds(pl.multiple_of(me * COLS, COLS), COLS)], tok.at[me], load_sem.at[6]
        ),
    ]
    for load in loads:
        load.start()

    pl.semaphore_wait(barrier, len(devs))

    c_copies = [
        remote(cot_hbm, cot.at[me], c_send.at[k], c_recv.at[k], fs_dev(d))
        for k, d in enumerate((1, 3))
    ]

    f_copies = []
    for k, (origin, target, lo, n) in enumerate(((3, 1, 0, UPPER), (1, 3, UPPER, TOK - UPPER))):
        part = cot.at[peer(origin), pl.ds(lo, n)]
        f_copies.append(remote(part, part, f_send.at[k], f_recv.at[k], fs_dev(target)))

    def token_copy(k, d, c):
        lo, n = T_CUTS[c]
        start = pl.multiple_of(peer(d) * COLS + lo, WIDTH)
        return remote(
            tok_hbm.at[:, pl.ds(start, n)],
            tok.at[me, :, pl.ds(lo, n)],
            t_send.at[k, c], t_recv.at[k, c], fs_dev(d),
        )

    def product_copy(k, d, c):
        lo, n = I_CUTS[c]
        start = pl.multiple_of(me * COLS + lo, WIDTH)
        return remote(
            ig.at[k, :, pl.ds(lo, n)],
            ig_out.at[:, pl.ds(start, n)],
            i_send.at[k, c], i_recv.at[k, c], fs_dev(d),
        )

    t_copies = [[token_copy(k, d, c) for k, d in enumerate(ORDER)] for c in range(len(T_CUTS))]
    i_copies = [[product_copy(k, d, c) for k, d in enumerate(ORDER)] for c in range(len(I_CUTS))]

    a_copies, b_copies, gb_copies, ga_copies = [], [], [], []
    for k in range(1, GA):
        rows = pl.ds(pl.multiple_of(a_peer(k) * RA, RA), RA)
        a_copies.append(remote(
            deq.at[rows], part_a.at[k - 1], a_send.at[k - 1], a_recv.at[k - 1], a_dev(k)
        ))
        ga_copies.append(remote(
            sum_a, full_a.at[a_id], ga_send.at[k - 1], ga_recv.at[k - 1], a_dev(k)
        ))
    for k in range(1, GB):
        b_copies.append(remote(
            mine_b.at[b_peer(k)], part_b.at[k - 1], b_send.at[k - 1], b_recv.at[k - 1], b_dev(k)
        ))
        gb_copies.append(remote(
            sum_b, full_b.at[b_id], gb_send.at[k - 1], gb_recv.at[k - 1], b_dev(k)
        ))

    r_copies = a_copies + b_copies + gb_copies + ga_copies

    def start(copies):
        for copy in copies:
            copy.start()

    def arrived(copies):
        for copy in copies:
            copy.wait_recv()

    def sent(copies):
        for copy in copies:
            copy.wait_send()

    def product(d, c):
        return lax.dot_general(
            cot[peer(d)], kp[pl.ds(c * WIDTH, WIDTH), :], (((1,), (1,)), ((), ())),
            preferred_element_type=jnp.float32,
        ).astype(jnp.bfloat16)

    def products(k):
        for c in range(CHUNKS):
            ig[k, :, pl.ds(c * WIDTH, WIDTH)] = product(ORDER[k], c)

    def own_product():
        for c in range(CHUNKS):
            first = pl.multiple_of(me * COLS + c * WIDTH, WIDTH)
            ig_out[:, pl.ds(first, WIDTH)] = product(0, c)

    def projection(c):
        arrived(t_copies[c])
        lo, n = T_CUTS[c]
        for at_col in range(lo, lo + n, WIDTH):
            cols = pl.ds(at_col, WIDTH)
            gp_out[cols, :] = lax.dot_general(
                tok[:, :, cols].reshape(NF * TOK, WIDTH), cot[...].reshape(NF * TOK, KV),
                (((0,), (0,)), ((), ())), preferred_element_type=jnp.float32,
            ).astype(jnp.bfloat16)

    def dequantize():
        loads[2].wait()
        loads[3].wait()
        spread = jnp.transpose(jnp.broadcast_to(scales[...], (BLOCK, ROWS)))
        deq[...] = codes[...].astype(jnp.float32) * spread
        start(a_copies)

    def sum_first():
        arrived(a_copies)
        total = deq[pl.ds(pl.multiple_of(a_id * RA, RA), RA)]
        for k in range(GA - 1):
            total = total + part_a[k]
        for b in range(GB):
            mine_b[b] = total[b * RB:(b + 1) * RB]
        start(b_copies)

    def sum_second():
        arrived(b_copies)
        total = mine_b[b_id]
        for k in range(GB - 1):
            total = total + part_b[k]
        sum_b[...] = total
        full_b[b_id] = total
        start(gb_copies)

    def gather_first():
        arrived(gb_copies)
        for b in range(GB):
            sum_a[b * RB:(b + 1) * RB] = full_b[b]
        full_a[a_id] = sum_a[...]
        start(ga_copies)

    def outer_step():
        loads[4].wait()
        loads[5].wait()
        arrived(ga_copies)
        delta = full_a[...].reshape(ROWS, BLOCK) / (GA * GB)
        moment_next = OUTER_MOMENTUM * moment[...] + delta
        np_out[...] = params[...] - OUTER_RATE * (delta + OUTER_MOMENTUM * moment_next)
        nm_out[...] = moment_next

    start(c_copies)
    start(t_copies[0])
    dequantize()
    arrived(c_copies)
    start(f_copies)
    start(t_copies[1])
    sum_first()
    loads[0].wait()
    loads[1].wait()
    products(1)
    products(2)
    sum_second()
    start(t_copies[2])
    gather_first()
    arrived(f_copies)
    products(0)
    own_product()
    start(t_copies[3])
    outer_step()
    start(i_copies[0])
    loads[6].wait()
    projection(0)
    projection(1)
    projection(2)
    projection(3)
    for row in i_copies:
        arrived(row)
    sent(c_copies + f_copies + r_copies)
    for row in t_copies:
        sent(row)
    for row in i_copies:
        sent(row)

def finish(*refs):
    n = len(refs) // 2
    sems = refs[-1]
    copies = [pltpu.make_async_copy(refs[k], refs[n + k], sems.at[k]) for k in range(n)]
    for copy in copies:
        copy.start()
    for copy in copies:
        copy.wait()


def local(tokens, key_proj, cotangent, codes, block_scales, outer_params, outer_moment):
    f32, bf16 = jnp.float32, jnp.bfloat16
    any_spec = pl.BlockSpec(memory_space=pl.ANY)
    hbm_spec = pl.BlockSpec(memory_space=pltpu.HBM)
    vmem_spec = pl.BlockSpec(memory_space=pltpu.VMEM)
    dma = pltpu.SemaphoreType.DMA
    vmem = pltpu.VMEM
    results = pl.pallas_call(
        kernel,
        out_shape=(
            pltpu.VMEM((COLS, KV), bf16),
            pltpu.VMEM((TOK, NF * COLS), bf16),
            pltpu.VMEM((ROWS, BLOCK), f32),
            pltpu.VMEM((ROWS, BLOCK), f32),
        ),
        in_specs=[hbm_spec] * 7,
        out_specs=(vmem_spec,) * 4,
        scratch_shapes=[
            vmem((NF, TOK, COLS), bf16),
            vmem((COLS, KV), bf16),
            vmem((NF, TOK, KV), bf16),
            vmem((NF - 1, TOK, COLS), bf16),
            vmem((ROWS, BLOCK), jnp.int32),
            vmem((1, ROWS), f32),
            vmem((ROWS, BLOCK), f32),
            vmem((ROWS, BLOCK), f32),
            vmem((ROWS, BLOCK), f32),
            vmem((GA - 1, RA, BLOCK), f32),
            vmem((GB, RB, BLOCK), f32),
            vmem((GB - 1, RB, BLOCK), f32),
            vmem((RB, BLOCK), f32),
            vmem((GB, RB, BLOCK), f32),
            vmem((RA, BLOCK), f32),
            vmem((GA, RA, BLOCK), f32),
            dma((7,)),
            dma((2,)), dma((2,)), dma((2,)), dma((2,)),
            dma((3, len(T_CUTS))), dma((3, len(T_CUTS))),
            dma((3, len(I_CUTS))), dma((3, len(I_CUTS))),
            dma((GA - 1,)), dma((GA - 1,)), dma((GB - 1,)), dma((GB - 1,)),
            dma((GB - 1,)), dma((GB - 1,)), dma((GA - 1,)), dma((GA - 1,)),
        ],
        compiler_params=pltpu.CompilerParams(
            collective_id=0, has_side_effects=True, vmem_limit_bytes=48 * 1024 * 1024
        ),
        name="step",
    )(
        tokens[0], key_proj[0], cotangent[0], codes.reshape(ROWS, BLOCK), block_scales,
        outer_params.reshape(ROWS, BLOCK), outer_moment.reshape(ROWS, BLOCK),
    )
    grad_proj, input_grad, new_params, new_moment = pl.pallas_call(
        finish,
        out_shape=tuple(pltpu.HBM(r.shape, r.dtype) for r in results),
        in_specs=[any_spec] * 4,
        out_specs=(hbm_spec,) * 4,
        scratch_shapes=[dma((4,))],
        compiler_params=pltpu.CompilerParams(vmem_limit_bytes=8 * 1024 * 1024),
        name="finish",
    )(*results)
    return grad_proj[None], input_grad[None], new_params.reshape(-1), new_moment.reshape(-1)


def solution(mesh):
    return jax.shard_map(
        local,
        mesh=mesh,
        in_specs=(
            P("rep", "fsdp", None),
            P("rep", "fsdp", None),
            P("rep", "fsdp", None),
            P("rep", "fsdp"),
            P("rep", "fsdp"),
            P("fsdp"),
            P("fsdp"),
        ),
        out_specs=(P("rep", "fsdp", None), P("rep", "fsdp", None), P("fsdp"), P("fsdp")),
        check_vma=False,
    )
```

time: 214 us -> 203 us (0.949)
  local copies, waits for them, and re-layouts: 6.46 us -> 0 us
  Pallas kernels: 207 us -> 201 us
    pallas_call x1 -> x2, Pallas kernels: 207 us -> 201 us  [the longest x1 198 us: local(): pl.pallas_call(kernel, out_shape=(pltpu.VMEM((COLS, KV), bf16), pltpu.VME...]
    unnamed x10 -> x0, local copies, waits for them, and re-layouts: 6.46 us -> none
where the time goes in v2:
time: 203 us; the launch traced here: 201 us
  Pallas kernels  201 us (99%)
    pallas_call x1, Pallas kernels, local(): pl.pallas_call(kernel, out_shape=(pltpu.VMEM((COLS, KV), bf16), pltpu.VME...  198 us

profile of v2, /device:TPU:1, one launch (start us, length us, event | category | flops | bytes accessed | tf_op | source)
XLA Modules:
  0.0 201.4 jit_solution(4968578026688684480)
XLA Ops:
  0.6 198.1 %step.1 = (bf16[2048,512]{1,0:T(8,128)(2,1)S(1)}, bf16[240,8192]{1,0:T(8,128)(2,1)S(1)}, f32[256,128]{1,0:T(8,128)S(1)}, f32[256,128]{1,0:T(8,128)S(1)}) custom-call(bf16[240,8192]{1,0:T(8,128)(2,1)} %bitcast.10, bf16[2048,512]{1,0:T(8,128)(2,1)} %bitcast.11, bf16[240,512]{1,0:T(8,128)(2,1)} %bitcast.12, s32[256,128]{1,0:T(8,128)} %bitcast.13, ...), custom_call_target="tpu_custom_call" | custom-call | tf_op jit(solution)/shard_map/step/pallas_call | solution.py:273
  198.7 2.7 %finish.1 = (bf16[2048,512]{1,0:T(8,128)(2,1)}, bf16[240,8192]{1,0:T(8,128)(2,1)}, f32[256,128]{1,0:T(8,128)}, f32[256,128]{1,0:T(8,128)}) custom-call(bf16[2048,512]{1,0:T(8,128)(2,1)S(1)} %get-tuple-element.12.refs_0_, bf16[240,8192]{1,0:T(8,128)(2,1)S(1)} %get-tuple-element.13.refs_1_, f32[256,128]{1,0:T(8,128)S(1)} %get-tuple-element.14.refs_2_, ...), custom_call_target="tpu_custom_call" | custom-call | tf_op jit(solution)/shard_map/finish/pallas_call | solution.py:315

commit v3 on v2

--- a/solution.py
+++ b/solution.py
@@ -17,7 +17,7 @@
 
 WIDTH = 256
 CHUNKS = COLS // WIDTH
-T_CUTS = ((0, 256), (256, 256), (512, 256), (768, 1280))
+T_CUTS = ((0, 512), (512, 512), (1024, 1024))
 I_CUTS = ((0, 2048),)
 UPPER = 128
 ROWS = 256
@@ -226,25 +226,23 @@
     arrived(c_copies)
     start(f_copies)
     start(t_copies[1])
-    sum_first()
     loads[0].wait()
     loads[1].wait()
     products(1)
     products(2)
-    sum_second()
-    start(t_copies[2])
-    gather_first()
+    sum_first()
     arrived(f_copies)
     products(0)
+    start(t_copies[2])
+    sum_second()
+    start(i_copies[0])
     own_product()
-    start(t_copies[3])
+    gather_first()
     outer_step()
-    start(i_copies[0])
     loads[6].wait()
     projection(0)
     projection(1)
     projection(2)
-    projection(3)
     for row in i_copies:
         arrived(row)
     sent(c_copies + f_copies + r_copies)

time: 203 us -> 201 us (level)
  no operation moved by 1% of the time
where the time goes in v3:
time: 201 us
  Pallas kernels  200 us (100%)
    pallas_call x1, Pallas kernels, local(): pl.pallas_call(kernel, out_shape=(pltpu.VMEM((COLS, KV), bf16), pltpu.VME...  197 us

profile of v3, /device:TPU:1, one launch (start us, length us, event | category | flops | bytes accessed | tf_op | source)
XLA Modules:
  0.0 200.7 jit_solution(12384235437754121454)
XLA Ops:
  0.6 197.3 %step.1 = (bf16[2048,512]{1,0:T(8,128)(2,1)S(1)}, bf16[240,8192]{1,0:T(8,128)(2,1)S(1)}, f32[256,128]{1,0:T(8,128)S(1)}, f32[256,128]{1,0:T(8,128)S(1)}) custom-call(bf16[240,8192]{1,0:T(8,128)(2,1)} %bitcast.10, bf16[2048,512]{1,0:T(8,128)(2,1)} %bitcast.11, bf16[240,512]{1,0:T(8,128)(2,1)} %bitcast.12, s32[256,128]{1,0:T(8,128)} %bitcast.13, ...), custom_call_target="tpu_custom_call" | custom-call | tf_op jit(solution)/shard_map/step/pallas_call | solution.py:271
  198.0 2.7 %finish.1 = (bf16[2048,512]{1,0:T(8,128)(2,1)}, bf16[240,8192]{1,0:T(8,128)(2,1)}, f32[256,128]{1,0:T(8,128)}, f32[256,128]{1,0:T(8,128)}) custom-call(bf16[2048,512]{1,0:T(8,128)(2,1)S(1)} %get-tuple-element.12.refs_0_, bf16[240,8192]{1,0:T(8,128)(2,1)S(1)} %get-tuple-element.13.refs_1_, f32[256,128]{1,0:T(8,128)S(1)} %get-tuple-element.14.refs_2_, ...), custom_call_target="tpu_custom_call" | custom-call | tf_op jit(solution)/shard_map/finish/pallas_call | solution.py:313

commit v4 on v3

--- a/solution.py
+++ b/solution.py
@@ -17,7 +17,7 @@
 
 WIDTH = 256
 CHUNKS = COLS // WIDTH
-T_CUTS = ((0, 512), (512, 512), (1024, 1024))
+T_CUTS = ((0, 512), (512, 768), (1280, 768))
 I_CUTS = ((0, 2048),)
 UPPER = 128
 ROWS = 256
@@ -75,20 +75,6 @@
     devs += [b_dev(k) for k in range(1, GB)] + [a_dev(k) for k in range(1, GA)]
     for dev in devs:
         pl.semaphore_signal(barrier, inc=1, device_id=dev, device_id_type=MESH)
-
-    loads = [
-        pltpu.make_async_copy(cot_hbm, cot.at[me], load_sem.at[0]),
-        pltpu.make_async_copy(kp_hbm, kp, load_sem.at[1]),
-        pltpu.make_async_copy(codes_hbm, codes, load_sem.at[2]),
-        pltpu.make_async_copy(scales_hbm, scales, load_sem.at[3]),
-        pltpu.make_async_copy(params_hbm, params, load_sem.at[4]),
-        pltpu.make_async_copy(moment_hbm, moment, load_sem.at[5]),
-        pltpu.make_async_copy(
-            tok_hbm.at[:, pl.ds(pl.multiple_of(me * COLS, COLS), COLS)], tok.at[me], load_sem.at[6]
-        ),
-    ]
-    for load in loads:
-        load.start()
 
     pl.semaphore_wait(barrier, len(devs))
 
@@ -142,6 +128,18 @@
 
     r_copies = a_copies + b_copies + gb_copies + ga_copies
 
+    loads = [
+        pltpu.make_async_copy(cot_hbm, cot.at[me], load_sem.at[0]),
+        pltpu.make_async_copy(kp_hbm, kp, load_sem.at[1]),
+        pltpu.make_async_copy(codes_hbm, codes, load_sem.at[2]),
+        pltpu.make_async_copy(scales_hbm, scales, load_sem.at[3]),
+        pltpu.make_async_copy(params_hbm, params, load_sem.at[4]),
+        pltpu.make_async_copy(moment_hbm, moment, load_sem.at[5]),
+        pltpu.make_async_copy(
+            tok_hbm.at[:, pl.ds(pl.multiple_of(me * COLS, COLS), COLS)], tok.at[me], load_sem.at[6]
+        ),
+    ]
+
     def start(copies):
         for copy in copies:
             copy.start()
@@ -222,6 +220,9 @@
 
     start(c_copies)
     start(t_copies[0])
+    start(loads[2:4])
+    start(loads[:2])
+    start(loads[4:])
     dequantize()
     arrived(c_copies)
     start(f_copies)
@@ -243,11 +244,11 @@
     projection(0)
     projection(1)
     projection(2)
-    for row in i_copies:
-        arrived(row)
     sent(c_copies + f_copies + r_copies)
     for row in t_copies:
         sent(row)
+    for row in i_copies:
+        arrived(row)
     for row in i_copies:
         sent(row)
 

time: 201 us -> 200 us (level)
  no operation moved by 1% of the time
where the time goes in v4:
time: 200 us; the launch traced here: 199 us
  Pallas kernels  199 us (100%)
    pallas_call x1, Pallas kernels, local(): pl.pallas_call(kernel, out_shape=(pltpu.VMEM((COLS, KV), bf16), pltpu.VME...  196 us

profile of v4, /device:TPU:1, one launch (start us, length us, event | category | flops | bytes accessed | tf_op | source)
XLA Modules:
  0.0 199.4 jit_solution(6537723484338956314)
XLA Ops:
  0.6 196.0 %step.1 = (bf16[2048,512]{1,0:T(8,128)(2,1)S(1)}, bf16[240,8192]{1,0:T(8,128)(2,1)S(1)}, f32[256,128]{1,0:T(8,128)S(1)}, f32[256,128]{1,0:T(8,128)S(1)}) custom-call(bf16[240,8192]{1,0:T(8,128)(2,1)} %bitcast.10, bf16[2048,512]{1,0:T(8,128)(2,1)} %bitcast.11, bf16[240,512]{1,0:T(8,128)(2,1)} %bitcast.12, s32[256,128]{1,0:T(8,128)} %bitcast.13, ...), custom_call_target="tpu_custom_call" | custom-call | tf_op jit(solution)/shard_map/step/pallas_call | solution.py:272
  196.7 2.7 %finish.1 = (bf16[2048,512]{1,0:T(8,128)(2,1)}, bf16[240,8192]{1,0:T(8,128)(2,1)}, f32[256,128]{1,0:T(8,128)}, f32[256,128]{1,0:T(8,128)}) custom-call(bf16[2048,512]{1,0:T(8,128)(2,1)S(1)} %get-tuple-element.12.refs_0_, bf16[240,8192]{1,0:T(8,128)(2,1)S(1)} %get-tuple-element.13.refs_1_, f32[256,128]{1,0:T(8,128)S(1)} %get-tuple-element.14.refs_2_, ...), custom_call_target="tpu_custom_call" | custom-call | tf_op jit(solution)/shard_map/finish/pallas_call | solution.py:314

commit v5 on v4

--- a/solution.py
+++ b/solution.py
@@ -223,9 +223,9 @@
     start(loads[2:4])
     start(loads[:2])
     start(loads[4:])
-    dequantize()
     arrived(c_copies)
     start(f_copies)
+    dequantize()
     start(t_copies[1])
     loads[0].wait()
     loads[1].wait()

time: 200 us -> 200 us (level)
  no operation moved by 1% of the time
where the time goes in v5:
time: 200 us; the launch traced here: 199 us
  Pallas kernels  199 us (100%)
    pallas_call x1, Pallas kernels, local(): pl.pallas_call(kernel, out_shape=(pltpu.VMEM((COLS, KV), bf16), pltpu.VME...  196 us

profile of v5, /device:TPU:1, one launch (start us, length us, event | category | flops | bytes accessed | tf_op | source)
XLA Modules:
  0.0 199.4 jit_solution(10672624706936419377)
XLA Ops:
  0.6 196.0 %step.1 = (bf16[2048,512]{1,0:T(8,128)(2,1)S(1)}, bf16[240,8192]{1,0:T(8,128)(2,1)S(1)}, f32[256,128]{1,0:T(8,128)S(1)}, f32[256,128]{1,0:T(8,128)S(1)}) custom-call(bf16[240,8192]{1,0:T(8,128)(2,1)} %bitcast.10, bf16[2048,512]{1,0:T(8,128)(2,1)} %bitcast.11, bf16[240,512]{1,0:T(8,128)(2,1)} %bitcast.12, s32[256,128]{1,0:T(8,128)} %bitcast.13, ...), custom_call_target="tpu_custom_call" | custom-call | tf_op jit(solution)/shard_map/step/pallas_call | solution.py:272
  196.7 2.7 %finish.1 = (bf16[2048,512]{1,0:T(8,128)(2,1)}, bf16[240,8192]{1,0:T(8,128)(2,1)}, f32[256,128]{1,0:T(8,128)}, f32[256,128]{1,0:T(8,128)}) custom-call(bf16[2048,512]{1,0:T(8,128)(2,1)S(1)} %get-tuple-element.12.refs_0_, bf16[240,8192]{1,0:T(8,128)(2,1)S(1)} %get-tuple-element.13.refs_1_, f32[256,128]{1,0:T(8,128)S(1)} %get-tuple-element.14.refs_2_, ...), custom_call_target="tpu_custom_call" | custom-call | tf_op jit(solution)/shard_map/finish/pallas_call | solution.py:314
